TPU v7x, 32 devices: a whole 2x2x4 slice. The times are simulated.
32 devices in a mesh: groups: 2 (over y), tensor: 4 (over z), rows: 2 (over x), role: 2 (over core).
Axes of the slice: x: 2, y: 2, z: 4, core: 2. Of those that a mesh axis runs over, the one named last changes fastest.
Arguments:
- residual: bfloat16 [64, 8192], P(('groups', 'tensor'), ('rows', 'role')), parts along dimension 0, may hold values from -6 to 6
- attn_gain: float32 [8192], P(('rows', 'role')), may hold values from 0.1 to 1.9
- attn_proj: bfloat16 [3, 8192, 8192], P(None, ('rows', 'role'), 'tensor'), may hold values from -0.0625 to 0.0625
- cache_keys: bfloat16 [64, 32, 8192], P(('groups', 'rows', 'role'), None, 'tensor'), parts along dimension 0, may hold values from -600 to 600
- cache_values: bfloat16 [64, 32, 8192], P(('groups', 'rows', 'role'), None, 'tensor'), parts along dimension 0, may hold values from -6 to 6
- lengths: int32 [64], P(('groups', 'rows', 'role')), parts along dimension 0, may hold values from 1 to 32
- placement: int32 [64], P('groups'), parts along dimension 0, may hold values from 0 to 31, each once
- out_proj: bfloat16 [8192, 8192], P('tensor', ('rows', 'role')), may hold values from -0.0625 to 0.0625
- mix_gain: float32 [8192], P(('rows', 'role')), may hold values from 0.1 to 1.9
- mix_proj: bfloat16 [3, 8192, 8192], P(None, ('rows', 'role'), 'tensor'), may hold values from -0.0625 to 0.0625
- outer_taps: float32 [3, 3, 8192], P(None, None, 'tensor'), may hold values from -1 to 1
- outer_state: bfloat16 [2, 3, 64, 8192], P(None, None, ('groups', 'rows', 'role'), 'tensor'), parts along dimension 2, may hold values from -6 to 6
- inner_taps: float32 [3, 8192], P(None, 'tensor'), may hold values from -1 to 1
- inner_state: bfloat16 [2, 64, 8192], P(None, ('groups', 'rows', 'role'), 'tensor'), parts along dimension 1, may hold values from -6 to 6
Outputs:
- attended: bfloat16 [64, 8192], P(('groups', 'tensor'), ('rows', 'role')), parts along dimension 0
- gated: bfloat16 [64, 8192], P(('groups', 'rows', 'role'), 'tensor'), parts along dimension 0
There are 2 independent parts, one for each index of `groups`. A program takes and returns all parts, laid end to end along the dimension named above; an argument that names none is the same for every part. Nothing has to cross between parts.
Inputs may be any that keep to these rules, and one draw needn't show every extreme that they name: Cache slot s holds lengths[s] cached positions, the first of its 32. `placement`: each row has its own cache slot.
All inputs are finite; a program needn't handle non-finite values.
Results may differ from a plain program's by a relative error of at most 0.017.
Values may be sent and summed in bfloat16 or wider, within the bound.
A program may use at most 128 MiB of HBM per device.

v0:
```python
import math

import jax
import jax.numpy as jnp
from jax import lax
from jax.sharding import PartitionSpec as P

D = 8192
HEAD_DIM = 128


def local(
    residual,
    attn_gain,
    attn_proj,
    cache_keys,
    cache_values,
    lengths,
    placement,
    out_proj,
    mix_gain,
    mix_proj,
    outer_taps,
    outer_state,
    inner_taps,
    inner_state,
):
    widened = residual.astype(jnp.float32)
    squares = lax.psum(jnp.sum(widened * widened, axis=1), ("rows", "role"))
    normed = (widened * lax.rsqrt(squares / D + 1e-05)[:, None] * attn_gain).astype(jnp.bfloat16)
    terms = jnp.einsum(
        "rd,jde->jre",
        lax.all_gather(normed, "tensor", axis=0, tiled=True),
        attn_proj,
        preferred_element_type=jnp.float32,
    )
    row_total = placement.shape[0]
    slot_count = lengths.shape[0]
    inverse = (
        jnp.zeros((row_total,), jnp.int32).at[placement].set(jnp.arange(row_total, dtype=jnp.int32))
    )
    full = lax.psum(terms, ("rows", "role"))
    first_slot = lax.axis_index(("rows", "role")) * slot_count
    owned_rows = lax.dynamic_slice_in_dim(inverse, first_slot, slot_count)
    sums = jnp.take(full, owned_rows, axis=1)
    triple = sums.astype(jnp.bfloat16)
    width_here = attn_proj.shape[2]
    head_count = width_here // HEAD_DIM
    positions = cache_keys.shape[1]
    query = triple[0].reshape(slot_count, head_count, HEAD_DIM)
    fresh_key = triple[1].reshape(slot_count, head_count, HEAD_DIM)
    fresh_value = triple[2].reshape(slot_count, head_count, HEAD_DIM)
    keys_local = cache_keys.reshape(slot_count, positions, head_count, HEAD_DIM)
    values_local = cache_values.reshape(slot_count, positions, head_count, HEAD_DIM)
    scale = 1.0 / math.sqrt(HEAD_DIM)
    scores = (
        jnp.einsum("shd,sphd->shp", query, keys_local, preferred_element_type=jnp.float32) * scale
    )
    own_score = (
        jnp.einsum("shd,shd->sh", query, fresh_key, preferred_element_type=jnp.float32) * scale
    )
    live = jnp.arange(positions, dtype=jnp.int32)[None, None, :] < lengths[:, None, None]
    top_score = jnp.maximum(jnp.max(jnp.where(live, scores, -jnp.inf), axis=2), own_score)
    probs = jnp.where(live, jnp.exp(scores - top_score[:, :, None]), 0.0)
    self_prob = jnp.exp(own_score - top_score)
    total = jnp.sum(probs, axis=2) + self_prob
    weights = (probs / total[:, :, None]).astype(jnp.bfloat16)
    self_weight = (self_prob / total).astype(jnp.bfloat16)
    mixed = jnp.einsum("shp,sphd->shd", weights, values_local, preferred_element_type=jnp.float32)
    mixed = mixed + self_weight.astype(jnp.float32)[:, :, None] * fresh_value.astype(jnp.float32)
    slot_out = mixed.reshape(slot_count, width_here).astype(jnp.bfloat16)
    slot_terms = jnp.dot(
        lax.all_gather(slot_out, ("rows", "role"), axis=0, tiled=True),
        out_proj,
        preferred_element_type=jnp.float32,
    )
    token_terms = jnp.take(slot_terms, placement, axis=0)
    head_sums = lax.psum_scatter(
        token_terms.astype(jnp.bfloat16), "tensor", scatter_dimension=0, tiled=True
    ).astype(jnp.float32)
    attended = (widened + head_sums).astype(jnp.bfloat16)
    attended_wide = attended.astype(jnp.float32)
    mix_squares = lax.psum(jnp.sum(attended_wide * attended_wide, axis=1), ("rows", "role"))
    mix_normed = (attended_wide * lax.rsqrt(mix_squares / D + 1e-05)[:, None] * mix_gain).astype(
        jnp.bfloat16
    )
    mix_terms = jnp.einsum(
        "rd,jde->jre",
        lax.all_gather(mix_normed, "tensor", axis=0, tiled=True),
        mix_proj,
        preferred_element_type=jnp.float32,
    )
    branches = lax.psum_scatter(
        mix_terms.astype(jnp.bfloat16), ("rows", "role"), scatter_dimension=1, tiled=True
    ).astype(jnp.float32)
    conv = (
        outer_taps[0][:, None, :] * branches
        + outer_taps[1][:, None, :] * outer_state[0].astype(jnp.float32)
        + outer_taps[2][:, None, :] * outer_state[1].astype(jnp.float32)
    )
    product = conv[0] * conv[2]
    filtered = (
        inner_taps[0] * product
        + inner_taps[1] * inner_state[0].astype(jnp.float32)
        + inner_taps[2] * inner_state[1].astype(jnp.float32)
    )
    gated = (conv[1] * filtered).astype(jnp.bfloat16)
    return (attended, gated)


def solution(mesh):
    return jax.shard_map(
        local,
        mesh=mesh,
        in_specs=(
            P(("groups", "tensor"), ("rows", "role")),
            P(("rows", "role")),
            P(None, ("rows", "role"), "tensor"),
            P(("groups", "rows", "role"), None, "tensor"),
            P(("groups", "rows", "role"), None, "tensor"),
            P(("groups", "rows", "role")),
            P("groups"),
            P("tensor", ("rows", "role")),
            P(("rows", "role")),
            P(None, ("rows", "role"), "tensor"),
            P(None, None, "tensor"),
            P(None, None, ("groups", "rows", "role"), "tensor"),
            P(None, "tensor"),
            P(None, ("groups", "rows", "role"), "tensor"),
        ),
        out_specs=(
            P(("groups", "tensor"), ("rows", "role")),
            P(("groups", "rows", "role"), "tensor"),
        ),
        check_vma=False,
    )
```

profile of v0, /device:TPU:0, one launch (start us, length us, event | category | flops | bytes accessed | tf_op | source)
XLA Modules:
  0.0 157.6 jit_solution(4077247140797194828)
XLA Ops:
  7.2 0.7 compare_select_fusion.1
  8.0 0.7 compare_and_fusion.1
  8.6 0.9 fusion.15
  9.5 8.3 %psum.21 = f32[8]{0:T(128)S(1)} all-reduce(f32[8]{0:T(128)S(1)} %fusion.15), channel_id=1, replica_groups=mesh['groups'=2,'tensor'=4,'rows'=2,'role'=2] {'rows','role'}, use_global_device_ids=true, to_apply=%region_2.0 | all-reduce | flops 8 | bytes 64 | tf_op jit(solution)/shard_map/psum | solution.py:29
  17.9 0.8 fusion.17
  18.7 13.6 %all_gather.9 = bf16[32,2048]{1,0:T(8,128)(2,1)S(1)} all-gather(bf16[8,2048]{1,0:T(8,128)(2,1)S(1)} %fusion.17), channel_id=1, replica_groups=mesh['groups'=2,'tensor'=4,'rows'=2,'role'=2] {'tensor'}, dimensions={0}, use_global_device_ids=true | all-gather | bytes 163840 | tf_op jit(solution)/shard_map/all_gather | solution.py:33
  32.3 10.5 %convolution_bitcast_fusion = f32[3,32,2048]{2,1,0:T(8,128)S(1)} fusion(bf16[3,2048,2048]{2,1,0:T(8,128)(2,1)} %param.16, bf16[32,2048]{1,0:T(8,128)(2,1)S(1)} %all_gather.9), kind=kOutput, calls=%fused_computation.3 | convolution fusion | flops 805306368 | bytes 26083328 | tf_op jit(solution)/shard_map/rd,jde->jre/dot_general | solution.py:31
  42.8 18.9 %all-reduce.1 = bf16[3,32,2048]{2,1,0:T(8,128)(2,1)S(1)} all-reduce(f32[3,32,2048]{2,1,0:T(8,128)S(1)} %convolution_bitcast_fusion), channel_id=1, replica_groups=mesh['groups'=2,'tensor'=4,'rows'=2,'role'=2] {'rows','role'}, use_global_device_ids=true, to_apply=%region_3.0 | all-reduce | flops 196608 | bytes 1179648 | tf_op jit(solution)/shard_map/psum | solution.py:42
  62.1 0.7 scatter_custom_fusion
  62.9 0.7 gather_fusion
  64.1 0.6 fusion.4
  65.8 5.4 %all_gather.10 = bf16[32,2048]{1,0:T(8,128)(2,1)S(1)} all-gather(bf16[8,2048]{1,0:T(8,128)(2,1)S(1)} %bitcast.101), channel_id=1, replica_groups=mesh['groups'=2,'tensor'=4,'rows'=2,'role'=2] {'rows','role'}, dimensions={0}, use_global_device_ids=true | all-gather | bytes 163840 | tf_op jit(solution)/shard_map/all_gather | solution.py:73
  71.2 4.9 %fusion.38 = bf16[32,2048]{1,0:T(8,128)(2,1)S(1)} fusion(bf16[32,2048]{1,0:T(8,128)(2,1)S(1)} %all_gather.10, bf16[2048,2048]{1,0:T(8,128)(2,1)} %param.21), kind=kOutput, calls=%fused_computation.79 | convolution fusion | flops 268435456 | bytes 8650752 | tf_op jit(solution)/shard_map/dot_general | solution.py:72
  76.2 0.7 gather_fusion.1
  76.8 0.7 select_convert_fusion.1
  77.6 19.7 %reduce-scatter.5.cloned.1.call-done = bf16[8,2048]{1,0:T(8,128)(2,1)} async-done(((bf16[32,2048]{1,0:T(8,128)(2,1)}), bf16[8,2048]{1,0:T(8,128)(2,1)}) %reduce-scatter.5.cloned.1.call-update) | async-done | bytes 32784 | tf_op jit(solution)/shard_map/reduce_scatter | solution.py:78
  97.3 0.9 fusion.12
  98.2 5.7 %psum.23 = f32[8]{0:T(128)S(1)} all-reduce(f32[8]{0:T(128)S(1)} %get-tuple-element.4), channel_id=1, replica_groups=mesh['groups'=2,'tensor'=4,'rows'=2,'role'=2] {'rows','role'}, use_global_device_ids=true, to_apply=%region_8.9 | all-reduce | flops 8 | bytes 64 | tf_op jit(solution)/shard_map/psum | solution.py:83
  104.0 13.5 %all_gather.11 = bf16[32,2048]{1,0:T(8,128)(2,1)S(1)} all-gather(bf16[8,2048]{1,0:T(8,128)(2,1)S(1)} %fusion.14), channel_id=1, replica_groups=mesh['groups'=2,'tensor'=4,'rows'=2,'role'=2] {'tensor'}, dimensions={0}, use_global_device_ids=true | all-gather | bytes 163840 | tf_op jit(solution)/shard_map/all_gather | solution.py:89
  117.5 10.5 %fusion = bf16[3,32,2048]{2,1,0:T(8,128)(2,1)S(1)} fusion(bf16[3,2048,2048]{2,1,0:T(8,128)(2,1)} %param.23, bf16[32,2048]{1,0:T(8,128)(2,1)S(1)} %all_gather.11), kind=kOutput, calls=%fused_computation.5 | convolution fusion | flops 805502976 | bytes 25690112 | tf_op jit(solution)/shard_map/rd,jde->jre/dot_general | solution.py:87
  128.4 1.0 copy.39
  129.5 19.4 %reduce-scatter.7.cloned.1.call-done = bf16[8,6144]{1,0:T(8,128)(2,1)} async-done(((bf16[32,6144]{1,0:T(8,128)(2,1)}), bf16[8,6144]{1,0:T(8,128)(2,1)}) %reduce-scatter.7.cloned.1.call-update) | async-done | bytes 98320
  149.0 1.0 reshape.108
  150.1 0.7 fusion.24
  (48 shorter events, 2.8 us)
Async XLA Ops:
  7.2 58.2 %copy-start = (bf16[8,32,2048]{2,1,0:T(8,128)(2,1)S(1)}, bf16[8,32,2048]{2,1,0:T(8,128)(2,1)}, u32[]{:S(2)}) copy-start(bf16[8,32,2048]{2,1,0:T(8,128)(2,1)} %param.18) | copy-start | bytes 3145732
  7.2 90.1 %reduce-scatter.5.cloned.1.call-start = ((), (), s32[]{:S(2)}) async-start(), calls=%async_computation.2 | async-start | bytes 163840 | tf_op jit(solution)/shard_map/reduce_scatter | solution.py:78
  32.3 31.7 %copy-start.8 = (bf16[8,32,2048]{2,1,0:T(8,128)(2,1)S(1)}, bf16[8,32,2048]{2,1,0:T(8,128)(2,1)}, u32[]{:S(2)}) copy-start(bf16[8,32,2048]{2,1,0:T(8,128)(2,1)} %param.17) | copy-start | bytes 3145732
  32.3 32.4 %copy-start.9 = (s32[8]{0:T(128)S(1)}, s32[8]{0:T(128)}, u32[]{:S(2)}) copy-start(s32[8]{0:T(128)} %param.19) | copy-start | bytes 100
  32.3 65.0 %copy-start.1 = (bf16[8,2048]{1,0:T(8,128)(2,1)S(1)}, bf16[8,2048]{1,0:T(8,128)(2,1)}, u32[]{:S(2)}) copy-start(bf16[8,2048]{1,0:T(8,128)(2,1)} %param.14) | copy-start | bytes 98308
  32.3 71.6 %copy-start.7 = (f32[2048]{0:T(1024)S(1)}, f32[2048]{0:T(1024)}, u32[]{:S(2)}) copy-start(f32[2048]{0:T(1024)} %param.22) | copy-start | bytes 24580
  77.6 71.4 %reduce-scatter.7.cloned.1.call-start = ((), (), s32[]{:S(2)}) async-start(), calls=%async_computation.3 | async-start | bytes 491520
  98.2 31.2 %copy-start.3 = (bf16[8,2048]{1,0:T(8,128)(2,1)}, bf16[8,2048]{1,0:T(8,128)(2,1)S(1)}, u32[]{:S(2)}) copy-start(bf16[8,2048]{1,0:T(8,128)(2,1)S(1)} %get-tuple-element.5) | copy-start | bytes 98308
  117.5 12.0 %copy-start.6 = (f32[3,2048]{1,0:T(4,128)S(1)}, f32[3,2048]{1,0:T(4,128)}, u32[]{:S(2)}) copy-start(f32[3,2048]{1,0:T(4,128)} %param.26) | copy-start | bytes 73732
  117.5 12.0 %copy-start.4 = (f32[3,3,2048]{2,1,0:T(4,128)S(1)}, f32[3,3,2048]{2,1,0:T(4,128)}, u32[]{:S(2)}) copy-start(f32[3,3,2048]{2,1,0:T(4,128)} %param.24) | copy-start | bytes 221188
  117.5 32.5 %copy-start.2 = (bf16[2,3,8,2048]{3,2,1,0:T(8,128)(2,1)S(1)}, bf16[2,3,8,2048]{3,2,1,0:T(8,128)(2,1)}, u32[]{:S(2)}) copy-start(bf16[2,3,8,2048]{3,2,1,0:T(8,128)(2,1)} %param.25) | copy-start | bytes 589828
  117.5 32.7 %copy-start.5 = (bf16[2,8,2048]{2,1,0:T(8,128)(2,1)S(1)}, bf16[2,8,2048]{2,1,0:T(8,128)(2,1)}, u32[]{:S(2)}) copy-start(bf16[2,8,2048]{2,1,0:T(8,128)(2,1)} %param.27) | copy-start | bytes 196612
Sparse Core Ops, SparseCore 0:
  77.7 19.5 reduce-scatter.4
  129.6 19.3 reduce-scatter.6
where the time goes:
time: 158 us
  blocking collectives  65.4 us (41%)
  waiting for transfers between devices  39.1 us (25%)
  matrix products  27 us (17%)
  between operations  14.3 us (9%)
  other arithmetic  6.88 us (4%)
  local copies, waits for them, and re-layouts  4.83 us (3%)
    reduce_scatter x1, waiting for transfers between devices, local(): lax.psum_scatter(token_terms.astype(jnp.bfloat16), 'tensor', scatter_dime...  19.7 us
    unnamed x3, waiting for transfers between devices  19.5 us
    psum x1, blocking collectives, local(): full = lax.psum(terms, ('rows', 'role'))  18.9 us
    all_gather x1, blocking collectives, local(): lax.all_gather(normed, 'tensor', axis=0, tiled=True)  13.6 us
    all_gather x1, blocking collectives, local(): lax.all_gather(mix_normed, 'tensor', axis=0, tiled=True)  13.5 us
    dot_general x1, matrix products, local(): jnp.einsum('rd,jde->jre', lax.all_gather(mix_normed, 'tensor', axis=0, ti...  10.5 us
    dot_general x1, matrix products, local(): jnp.einsum('rd,jde->jre', lax.all_gather(normed, 'tensor', axis=0, tiled=...  10.5 us
    psum x1, blocking collectives, local(): squares = lax.psum(jnp.sum(widened * widened, axis=1), ('rows', 'role'))  8.34 us
  transfers between devices with their start and end apart: 2, of which 2 were waited for; matrix products, arithmetic and copies ran while one was open for 0% of the time, Pallas kernels for 0%

commit v1 on v0

v1 whole, which is shorter than its diff:
```python
import functools
import math

import jax
import jax.numpy as jnp
from jax import lax
from jax.experimental import pallas as pl
from jax.experimental.pallas import tpu as pltpu
from jax.sharding import PartitionSpec as P

HEAD_DIM = 128
LANES = 128
COLUMNS = 256
MESH = pl.DeviceIdType.MESH
F32 = jnp.float32
BF16 = jnp.bfloat16


def quotient(a, n):
    if n & (n - 1) == 0:
        return lax.shift_right_logical(a, jnp.int32(n.bit_length() - 1))
    return lax.div(a, jnp.int32(n))


def iota(shape, axis):
    return lax.broadcasted_iota(jnp.int32, shape, axis)


def flag(mask):
    return jnp.where(mask, 1.0, 0.0).astype(BF16)


def matmul(a, b):
    return jnp.dot(a, b, preferred_element_type=F32)


def matmul_nt(a, b):
    return lax.dot_general(a, b, (((1,), (1,)), ((), ())), preferred_element_type=F32)


def matmul_tn(a, b):
    return lax.dot_general(a, b, (((0,), (0,)), ((), ())), preferred_element_type=F32)


def kernel(
    nt,
    nr,
    nc,
    x_hbm,
    again_hbm,
    aproj_hbm,
    keys_hbm,
    vals_hbm,
    lens_ref,
    place_row_ref,
    oproj_hbm,
    mgain_hbm,
    mproj_hbm,
    otaps_hbm,
    ostate_hbm,
    itaps_hbm,
    istate_hbm,
    att_ref,
    gated_ref,
    xv,
    gainv,
    mgainv,
    wa,
    wo,
    wm,
    kv,
    vv,
    otv,
    osv,
    itv,
    isv,
    sq_send,
    sq_recv,
    nbuf,
    tbuf,
    rbuf,
    hbuf,
    obuf,
    robuf,
    abuf,
    msq_send,
    msq_recv,
    mbuf,
    rmbuf,
    lsem,
    wsem,
    sq_sems,
    n_sems,
    t_sems,
    h_sems,
    o_sems,
    a_sems,
    msq_sems,
    m_sems,
):
    ng = nr * nc
    me_t = lax.axis_index("tensor")
    me_g = lax.axis_index("rows") * nc + lax.axis_index("role")
    xb, feat = xv.shape
    width = wa.shape[2]
    slots, ctx = kv.shape[0], kv.shape[1]
    heads = width // HEAD_DIM
    batch = nt * xb
    total_feat = feat * ng

    def t_peer(k):
        return lax.rem(me_t + k, nt)

    def g_peer(k):
        return lax.rem(me_g + k, ng)

    def t_id(k):
        return {"tensor": t_peer(k)}

    def g_id(k):
        p = g_peer(k)
        return {"rows": lax.div(p, nc), "role": lax.rem(p, nc)}

    def remote(src, dst, sems, at, device):
        return pltpu.make_async_remote_copy(
            src_ref=src,
            dst_ref=dst,
            send_sem=sems.at[(0,) + at],
            recv_sem=sems.at[(1,) + at],
            device_id=device,
            device_id_type=MESH,
        )

    barrier = pltpu.get_barrier_semaphore()
    for k in range(1, nt):
        pl.semaphore_signal(barrier, inc=1, device_id=t_id(k), device_id_type=MESH)
    for k in range(1, ng):
        pl.semaphore_signal(barrier, inc=1, device_id=g_id(k), device_id_type=MESH)

    small = [
        pltpu.make_async_copy(s, d, lsem.at[i])
        for i, (s, d) in enumerate(
            [
                (x_hbm, xv),
                (again_hbm, gainv),
                (mgain_hbm, mgainv),
                (keys_hbm, kv),
                (vals_hbm, vv),
                (otaps_hbm, otv),
                (ostate_hbm, osv),
                (itaps_hbm, itv),
                (istate_hbm, isv),
            ]
        )
    ]
    a_copies = [pltpu.make_async_copy(aproj_hbm.at[j], wa.at[j], wsem.at[j]) for j in range(3)]
    o_copy = pltpu.make_async_copy(oproj_hbm, wo, wsem.at[3])
    m_homes = [wm, wa.at[0], wa.at[1]]
    m_copies = [
        pltpu.make_async_copy(mproj_hbm.at[j], m_homes[j], wsem.at[4 + j]) for j in range(3)
    ]
    small[0].start()
    small[1].start()
    for c in a_copies:
        c.start()
    for c in small[2:]:
        c.start()
    o_copy.start()
    m_copies[0].start()

    small[0].wait()
    small[1].wait()
    x = xv[...].astype(F32)
    sq_send[...] = jnp.broadcast_to(jnp.sum(x * x, axis=1, keepdims=True), sq_send.shape)
    pl.semaphore_wait(barrier, (nt - 1) + (ng - 1))
    pending = []
    copies = [remote(sq_send, sq_recv.at[k - 1], sq_sems, (k - 1,), g_id(k)) for k in range(1, ng)]
    for c in copies:
        c.start()
    pending += copies
    for c in copies:
        c.wait_recv()
    squares = sq_send[...]
    for k in range(ng - 1):
        squares = squares + sq_recv[k]
    scale_rows = lax.rsqrt(squares[:, :1] / total_feat + 1e-05)
    nbuf[me_t] = (x * scale_rows * gainv[...]).astype(BF16)
    copies = [
        remote(nbuf.at[me_t], nbuf.at[me_t], n_sems, (k - 1,), t_id(k)) for k in range(1, nt)
    ]
    for c in copies:
        c.start()
    pending += copies

    place_row = place_row_ref[...]
    to_slots = flag(place_row == iota((batch, batch), 0))
    for c in copies:
        c.wait_recv()
    normed = nbuf[...].astype(F32).reshape(batch, feat).astype(BF16)
    normed = matmul(to_slots, normed).astype(BF16)

    cols = min(COLUMNS, width)
    t_copies = []
    for j in range(3):
        a_copies[j].wait()

        def attn_step(c, carry, j=j):
            at = pl.ds(pl.multiple_of(c * cols, cols), cols)
            term = matmul(normed, wa[j, :, at])
            for g in range(ng):
                tbuf[g, j, :, at] = term[g * slots : (g + 1) * slots]
            return carry

        lax.fori_loop(0, width // cols, attn_step, 0)
        if j < 2:
            m_copies[1 + j].start()
        step = [
            remote(tbuf.at[g_peer(k), j], rbuf.at[k - 1, j], t_sems, (k - 1, j), g_id(k))
            for k in range(1, ng)
        ]
        for c in step:
            c.start()
        t_copies.append(step)
        pending += step

    rows = slots * heads
    expand_mask = quotient(iota((rows, slots), 0), heads) == iota((rows, slots), 1)
    expand = flag(expand_mask)
    collapse = flag(quotient(iota((slots, rows), 1), heads) == iota((slots, rows), 0))
    row_at = iota((rows, width), 0)
    head_mask = quotient(iota((rows, width), 1), HEAD_DIM) == row_at - heads * quotient(row_at, heads)
    row_at = iota((rows, slots * ctx), 0)
    col_at = iota((rows, slots * ctx), 1)
    col_slot = quotient(col_at, ctx)
    row_length = jnp.sum(
        jnp.where(expand_mask, lens_ref[...].astype(F32), 0.0), axis=1, keepdims=True
    )
    live = (quotient(row_at, heads) == col_slot) & (
        (col_at - ctx * col_slot).astype(F32) < row_length
    )

    triple = []
    small[3].wait()
    small[4].wait()
    for j in range(3):
        for c in t_copies[j]:
            c.wait_recv()
        total = tbuf[me_g, j]
        for k in range(ng - 1):
            total = total + rbuf[k, j]
        triple.append(total.astype(BF16))
    query, fresh_key, fresh_value = triple

    scale = 1.0 / math.sqrt(HEAD_DIM)
    spread = jnp.where(head_mask, matmul(expand, query), 0.0).astype(BF16)
    scores = matmul_nt(spread, kv[...].reshape(slots * ctx, width)) * scale
    own = (
        jnp.sum(
            jnp.where(expand_mask, matmul_nt(spread, fresh_key), 0.0), axis=1, keepdims=True
        )
        * scale
    )
    top = jnp.maximum(jnp.max(jnp.where(live, scores, -jnp.inf), axis=1, keepdims=True), own)
    probs = jnp.where(live, jnp.exp(scores - top), 0.0)
    self_prob = jnp.exp(own - top)
    total = jnp.sum(probs, axis=1, keepdims=True) + self_prob
    weights = (probs / total).astype(BF16)
    self_weight = (self_prob / total).astype(BF16).astype(F32)
    mixed = matmul(weights, vv[...].reshape(slots * ctx, width))
    mixed = mixed + self_weight * matmul(expand, fresh_value)
    mixed = jnp.where(head_mask, mixed, 0.0).astype(BF16)
    hbuf[me_g] = matmul(collapse, mixed).astype(BF16)
    copies = [
        remote(hbuf.at[me_g], hbuf.at[me_g], h_sems, (k - 1,), g_id(k)) for k in range(1, ng)
    ]
    for c in copies:
        c.start()
    pending += copies
    o_copy.wait()
    for c in copies:
        c.wait_recv()
    heads_out = hbuf[...].astype(F32).reshape(batch, width).astype(BF16)
    heads_out = matmul_tn(to_slots, heads_out).astype(BF16)

    ocols = min(COLUMNS, feat)

    def out_step(c, carry):
        at = pl.ds(pl.multiple_of(c * ocols, ocols), ocols)
        term = matmul(heads_out, wo[:, at])
        for t in range(nt):
            obuf[t, :, at] = term[t * xb : (t + 1) * xb].astype(BF16)
        return carry

    lax.fori_loop(0, feat // ocols, out_step, 0)
    copies = [
        remote(obuf.at[t_peer(k)], robuf.at[k - 1], o_sems, (k - 1,), t_id(k))
        for k in range(1, nt)
    ]
    for c in copies:
        c.start()
    pending += copies
    for c in copies:
        c.wait_recv()
    head_sums = obuf[me_t].astype(F32)
    for k in range(nt - 1):
        head_sums = head_sums + robuf[k].astype(F32)
    attended = (xv[...].astype(F32) + head_sums).astype(BF16)
    att_ref[...] = attended
    abuf[me_t] = attended
    copies = [
        remote(abuf.at[me_t], abuf.at[me_t], a_sems, (k - 1,), t_id(k)) for k in range(1, nt)
    ]
    for c in copies:
        c.start()
    pending += copies
    small[2].wait()
    for c in copies:
        c.wait_recv()

    wide = abuf[...].astype(F32).reshape(batch, feat)
    squares = jnp.sum(wide * wide, axis=1, keepdims=True)
    for g in range(ng):
        msq_send[g] = jnp.broadcast_to(squares[g * slots : (g + 1) * slots], msq_send.shape[1:])
    msq_copies = [
        remote(msq_send.at[g_peer(k)], msq_recv.at[k - 1], msq_sems, (k - 1,), g_id(k))
        for k in range(1, ng)
    ]
    for c in msq_copies:
        c.start()
    pending += msq_copies
    gained = (wide * mgainv[...]).astype(BF16)

    m_steps = []
    for j in range(3):
        m_copies[j].wait()

        def mix_step(c, carry, j=j):
            at = pl.ds(pl.multiple_of(c * cols, cols), cols)
            weight = wm[:, at] if j == 0 else wa[j - 1, :, at]
            term = matmul(gained, weight)
            for g in range(ng):
                mbuf[g, j, :, at] = term[g * slots : (g + 1) * slots].astype(BF16)
            return carry

        lax.fori_loop(0, width // cols, mix_step, 0)
        step = [
            remote(mbuf.at[g_peer(k), j], rmbuf.at[k - 1, j], m_sems, (k - 1, j), g_id(k))
            for k in range(1, ng)
        ]
        for c in step:
            c.start()
        m_steps.append(step)
        pending += step

    for c in small[5:]:
        c.wait()
    for c in msq_copies:
        c.wait_recv()
    squares = msq_send[me_g]
    for k in range(ng - 1):
        squares = squares + msq_recv[k]
    scale_rows = lax.rsqrt(squares[:, :1] / total_feat + 1e-05)
    conv = []
    for j in range(3):
        for c in m_steps[j]:
            c.wait_recv()
        total = mbuf[me_g, j].astype(F32)
        for k in range(ng - 1):
            total = total + rmbuf[k, j].astype(F32)
        conv.append(
            otv[0, j : j + 1] * (total * scale_rows)
            + otv[1, j : j + 1] * osv[0, j].astype(F32)
            + otv[2, j : j + 1] * osv[1, j].astype(F32)
        )
    product = conv[0] * conv[2]
    filtered = (
        itv[0:1] * product + itv[1:2] * isv[0].astype(F32) + itv[2:3] * isv[1].astype(F32)
    )
    gated_ref[...] = (conv[1] * filtered).astype(BF16)
    for c in pending:
        c.wait_send()


def local(
    nt,
    nr,
    nc,
    residual,
    attn_gain,
    attn_proj,
    cache_keys,
    cache_values,
    lengths,
    placement,
    out_proj,
    mix_gain,
    mix_proj,
    outer_taps,
    outer_state,
    inner_taps,
    inner_state,
):
    ng = nr * nc
    xb, feat = residual.shape
    slots = lengths.shape[0]
    batch = placement.shape[0]
    width = attn_proj.shape[2]
    anywhere = pl.BlockSpec(memory_space=pl.ANY)
    vmem = pl.BlockSpec(memory_space=pltpu.VMEM)
    dma = pltpu.SemaphoreType.DMA
    others_g, others_t = max(ng - 1, 1), max(nt - 1, 1)
    weight_values = attn_proj.size + out_proj.size + mix_proj.size
    return pl.pallas_call(
        functools.partial(kernel, nt, nr, nc),
        out_shape=(
            jax.ShapeDtypeStruct((xb, feat), BF16),
            jax.ShapeDtypeStruct((slots, width), BF16),
        ),
        in_specs=[anywhere] * 5 + [vmem] * 2 + [anywhere] * 7,
        out_specs=(vmem, vmem),
        scratch_shapes=[
            pltpu.VMEM((xb, feat), BF16),
            pltpu.VMEM((1, feat), F32),
            pltpu.VMEM((1, feat), F32),
            pltpu.VMEM(attn_proj.shape, BF16),
            pltpu.VMEM(out_proj.shape, BF16),
            pltpu.VMEM(mix_proj.shape[1:], BF16),
            pltpu.VMEM(cache_keys.shape, BF16),
            pltpu.VMEM(cache_values.shape, BF16),
            pltpu.VMEM(outer_taps.shape, F32),
            pltpu.VMEM(outer_state.shape, BF16),
            pltpu.VMEM(inner_taps.shape, F32),
            pltpu.VMEM(inner_state.shape, BF16),
            pltpu.VMEM((xb, LANES), F32),
            pltpu.VMEM((others_g, xb, LANES), F32),
            pltpu.VMEM((nt, xb, feat), BF16),
            pltpu.VMEM((ng, 3, slots, width), F32),
            pltpu.VMEM((others_g, 3, slots, width), F32),
            pltpu.VMEM((ng, slots, width), BF16),
            pltpu.VMEM((nt, xb, feat), BF16),
            pltpu.VMEM((others_t, xb, feat), BF16),
            pltpu.VMEM((nt, xb, feat), BF16),
            pltpu.VMEM((ng, slots, LANES), F32),
            pltpu.VMEM((others_g, slots, LANES), F32),
            pltpu.VMEM((ng, 3, slots, width), BF16),
            pltpu.VMEM((others_g, 3, slots, width), BF16),
            dma((9,)),
            dma((7,)),
            dma((2, others_g)),
            dma((2, others_t)),
            dma((2, others_g, 3)),
            dma((2, others_g)),
            dma((2, others_t)),
            dma((2, others_t)),
            dma((2, others_g)),
            dma((2, others_g, 3)),
        ],
        compiler_params=pltpu.CompilerParams(
            collective_id=0, has_side_effects=True, vmem_limit_bytes=58 * 2**20
        ),
        cost_estimate=pl.CostEstimate(
            flops=2 * batch * weight_values, bytes_accessed=2 * weight_values, transcendentals=0
        ),
        name="hybrid_block",
    )(
        residual,
        attn_gain.reshape(1, feat),
        attn_proj,
        cache_keys,
        cache_values,
        lengths.reshape(1, slots),
        placement.reshape(1, batch),
        out_proj,
        mix_gain.reshape(1, feat),
        mix_proj,
        outer_taps,
        outer_state,
        inner_taps,
        inner_state,
    )


def solution(mesh):
    return jax.shard_map(
        functools.partial(local, mesh.shape["tensor"], mesh.shape["rows"], mesh.shape["role"]),
        mesh=mesh,
        in_specs=(
            P(("groups", "tensor"), ("rows", "role")),
            P(("rows", "role")),
            P(None, ("rows", "role"), "tensor"),
            P(("groups", "rows", "role"), None, "tensor"),
            P(("groups", "rows", "role"), None, "tensor"),
            P(("groups", "rows", "role")),
            P("groups"),
            P("tensor", ("rows", "role")),
            P(("rows", "role")),
            P(None, ("rows", "role"), "tensor"),
            P(None, None, "tensor"),
            P(None, None, ("groups", "rows", "role"), "tensor"),
            P(None, "tensor"),
            P(None, ("groups", "rows", "role"), "tensor"),
        ),
        out_specs=(
            P(("groups", "tensor"), ("rows", "role")),
            P(("groups", "rows", "role"), "tensor"),
        ),
        check_vma=False,
    )
```

time: 158 us -> 56.1 us (0.36)
  blocking collectives: 65.4 us -> 0 us
  Pallas kernels: 0 us -> 52.5 us
  waiting for transfers between devices: 39.1 us -> 0 us
  matrix products: 27 us -> 0 us
  between operations: 14.3 us -> 0.64 us
  other arithmetic: 6.88 us -> 0 us
  local copies, waits for them, and re-layouts: 4.83 us -> 2.75 us
    pallas_call x0 -> x1, Pallas kernels: none -> 52.5 us  [local(): pl.pallas_call(functools.partial(kernel, nt, nr, nc), out_shape=(jax.Shap...]
    psum x3 -> x0, blocking collectives: 32.9 us -> none  [the longest x1 18.9 us: local(): full = lax.psum(terms, ('rows', 'role'))]
    all_gather x3 -> x0, blocking collectives: 32.6 us -> none  [the longest x1 13.6 us: local(): lax.all_gather(normed, 'tensor', axis=0, tiled=True)]
    dot_general x5 -> x0, matrix products: 27 us -> none  [the longest x1 10.5 us: local(): jnp.einsum('rd,jde->jre', lax.all_gather(mix_normed, 'tensor', axis=0, ti...]
    reduce_scatter x1 -> x0, waiting for transfers between devices: 19.7 us -> none  [local(): lax.psum_scatter(token_terms.astype(jnp.bfloat16), 'tensor', scatter_dime...]
    unnamed x3 -> x0, waiting for transfers between devices: 19.5 us -> none
    convert_element_type x7 -> x0, other arithmetic: 2.53 us -> none  [the longest x1 0.84 us: local(): (widened * lax.rsqrt(squares / D + 1e-05)[:, None] * attn_gain).astype(jn...]
    reduce_sum x3 -> x0, other arithmetic: 1.95 us -> none  [the longest x1 0.89 us: local(): jnp.sum(attended_wide * attended_wide, axis=1)]
  transfers between devices with their start and end apart: 2 -> 0, of which waited for: 2 -> 0; matrix products, arithmetic and copies ran while one was open for 0% -> 0% of each run, Pallas kernels for 0% -> 0%
where the time goes in v1:
time: 56.1 us; the launch traced here: 55.8 us
  Pallas kernels  52.5 us (94%)
  local copies, waits for them, and re-layouts  2.75 us (5%)
  between operations  0.64 us (1%)
    pallas_call x1, Pallas kernels, local(): pl.pallas_call(functools.partial(kernel, nt, nr, nc), out_shape=(jax.Shap...  52.5 us
    unnamed x2, local copies, waits for them, and re-layouts  2.75 us

profile of v1, /device:TPU:0, one launch (start us, length us, event | category | flops | bytes accessed | tf_op | source)
XLA Modules:
  0.0 55.8 jit_solution(3662954487187324411)
XLA Ops:
  0.6 52.5 %hybrid_block.1 = (bf16[8,2048]{1,0:T(8,128)(2,1)}, bf16[8,2048]{1,0:T(8,128)(2,1)}) custom-call(bf16[8,2048]{1,0:T(8,128)(2,1)} %x_hbm.1, f32[1,2048]{1,0:T(1,128)} %bitcast.4, bf16[3,2048,2048]{2,1,0:T(8,128)(2,1)} %aproj_hbm.1, bf16[8,32,2048]{2,1,0:T(8,128)(2,1)} %keys_hbm.1, bf16[8,32,2048]{2,1,0:T(8,128)(2,1)} %vals_hbm.1, s32[1,8]{1,0:T(1,128)} %bitcast.6, ...), custom_call_target="tpu_custom_call" | custom-call | flops 1879048192 | bytes 58720256 | tf_op jit(solution)/shard_map/hybrid_block/pallas_call | solution.py:413
  53.1 1.4 %copy.18 = bf16[8,2048]{1,0:T(8,128)(2,1)} copy(bf16[8,2048]{1,0:T(8,128)(2,1)} %get-tuple-element.4) | data formatting | bytes 65536
  54.5 1.4 %copy.19 = bf16[8,2048]{1,0:T(8,128)(2,1)} copy(bf16[8,2048]{1,0:T(8,128)(2,1)} %get-tuple-element.5) | data formatting | bytes 65536

commit v2 on v1

--- a/solution.py
+++ b/solution.py
@@ -10,7 +10,7 @@
 
 HEAD_DIM = 128
 LANES = 128
-COLUMNS = 256
+COLUMNS = 1024
 MESH = pl.DeviceIdType.MESH
 F32 = jnp.float32
 BF16 = jnp.bfloat16
@@ -77,7 +77,10 @@
     sq_send,
     sq_recv,
     nbuf,
+    fbuf,
     tbuf,
+    cbuf,
+    sbuf,
     rbuf,
     hbuf,
     obuf,
@@ -91,6 +94,8 @@
     wsem,
     sq_sems,
     n_sems,
+    f_sems,
+    c_sems,
     t_sems,
     h_sems,
     o_sems,
@@ -100,7 +105,8 @@
 ):
     ng = nr * nc
     me_t = lax.axis_index("tensor")
-    me_g = lax.axis_index("rows") * nc + lax.axis_index("role")
+    me_r, me_c = lax.axis_index("rows"), lax.axis_index("role")
+    me_g = me_r * nc + me_c
     xb, feat = xv.shape
     width = wa.shape[2]
     slots, ctx = kv.shape[0], kv.shape[1]
@@ -120,6 +126,12 @@
     def g_id(k):
         p = g_peer(k)
         return {"rows": lax.div(p, nc), "role": lax.rem(p, nc)}
+
+    def r_peer(k):
+        return lax.rem(me_r + k, nr)
+
+    def c_peer(k):
+        return lax.rem(me_c + k, nc)
 
     def remote(src, dst, sems, at, device):
         return pltpu.make_async_remote_copy(
@@ -163,44 +175,63 @@
     small[1].start()
     for c in a_copies:
         c.start()
-    for c in small[2:]:
-        c.start()
-    o_copy.start()
-    m_copies[0].start()
+    for c in small[2:5]:
+        c.start()
 
     small[0].wait()
-    small[1].wait()
     x = xv[...].astype(F32)
     sq_send[...] = jnp.broadcast_to(jnp.sum(x * x, axis=1, keepdims=True), sq_send.shape)
+    nbuf[me_t] = xv[...]
     pl.semaphore_wait(barrier, (nt - 1) + (ng - 1))
     pending = []
     copies = [remote(sq_send, sq_recv.at[k - 1], sq_sems, (k - 1,), g_id(k)) for k in range(1, ng)]
-    for c in copies:
-        c.start()
-    pending += copies
+    n_copies = [remote(xv, nbuf.at[me_t], n_sems, (k - 1,), t_id(k)) for k in range(1, nt)]
+    for c in copies + n_copies:
+        c.start()
+    pending += copies + n_copies
+    place_row = place_row_ref[...]
+    to_slots = flag(place_row == iota((batch, batch), 0))
     for c in copies:
         c.wait_recv()
     squares = sq_send[...]
     for k in range(ng - 1):
         squares = squares + sq_recv[k]
-    scale_rows = lax.rsqrt(squares[:, :1] / total_feat + 1e-05)
-    nbuf[me_t] = (x * scale_rows * gainv[...]).astype(BF16)
-    copies = [
-        remote(nbuf.at[me_t], nbuf.at[me_t], n_sems, (k - 1,), t_id(k)) for k in range(1, nt)
+    fbuf[me_t] = lax.rsqrt(squares / total_feat + 1e-05)
+    f_copies = [
+        remote(fbuf.at[me_t], fbuf.at[me_t], f_sems, (k - 1,), t_id(k)) for k in range(1, nt)
     ]
-    for c in copies:
-        c.start()
-    pending += copies
-
-    place_row = place_row_ref[...]
-    to_slots = flag(place_row == iota((batch, batch), 0))
-    for c in copies:
+    for c in f_copies:
+        c.start()
+    pending += f_copies
+    small[1].wait()
+    for c in n_copies + f_copies:
         c.wait_recv()
-    normed = nbuf[...].astype(F32).reshape(batch, feat).astype(BF16)
-    normed = matmul(to_slots, normed).astype(BF16)
-
-    cols = min(COLUMNS, width)
-    t_copies = []
+    o_copy.start()
+    m_copies[0].start()
+    for c in small[5:]:
+        c.start()
+    factors = fbuf[...].reshape(batch, LANES)[:, :1]
+    normed = nbuf[...].astype(F32).reshape(batch, feat) * factors * gainv[...]
+    normed = matmul(to_slots, normed.astype(BF16)).astype(BF16)
+
+    cols = math.gcd(COLUMNS, width)
+
+    def exchange_chips(j):
+        for c in c_copies[j]:
+            c.wait_recv()
+        total = tbuf[j, me_c]
+        for k in range(nc - 1):
+            total = total + cbuf[k, j]
+        sbuf[j] = total
+        step = [
+            remote(sbuf.at[j, r_peer(k)], rbuf.at[k - 1, j], t_sems, (k - 1, j), {"rows": r_peer(k)})
+            for k in range(1, nr)
+        ]
+        for c in step:
+            c.start()
+        return step
+
+    c_copies, t_copies = [], []
     for j in range(3):
         a_copies[j].wait()
 
@@ -208,20 +239,33 @@
             at = pl.ds(pl.multiple_of(c * cols, cols), cols)
             term = matmul(normed, wa[j, :, at])
             for g in range(ng):
-                tbuf[g, j, :, at] = term[g * slots : (g + 1) * slots]
+                tbuf[j, g % nc, g // nc, :, at] = term[g * slots : (g + 1) * slots]
             return carry
 
         lax.fori_loop(0, width // cols, attn_step, 0)
         if j < 2:
             m_copies[1 + j].start()
         step = [
-            remote(tbuf.at[g_peer(k), j], rbuf.at[k - 1, j], t_sems, (k - 1, j), g_id(k))
-            for k in range(1, ng)
+            remote(tbuf.at[j, c_peer(k)], cbuf.at[k - 1, j], c_sems, (k - 1, j), {"role": c_peer(k)})
+            for k in range(1, nc)
         ]
         for c in step:
             c.start()
-        t_copies.append(step)
+        c_copies.append(step)
         pending += step
+        if j > 0:
+            t_copies.append(exchange_chips(j - 1))
+    t_copies.append(exchange_chips(2))
+    for step in t_copies:
+        pending += step
+
+    def projected(j):
+        for c in t_copies[j]:
+            c.wait_recv()
+        total = sbuf[j, me_r]
+        for k in range(nr - 1):
+            total = total + rbuf[k, j]
+        return total.astype(BF16)
 
     rows = slots * heads
     expand_mask = quotient(iota((rows, slots), 0), heads) == iota((rows, slots), 1)
@@ -239,24 +283,15 @@
         (col_at - ctx * col_slot).astype(F32) < row_length
     )
 
-    triple = []
     small[3].wait()
     small[4].wait()
-    for j in range(3):
-        for c in t_copies[j]:
-            c.wait_recv()
-        total = tbuf[me_g, j]
-        for k in range(ng - 1):
-            total = total + rbuf[k, j]
-        triple.append(total.astype(BF16))
-    query, fresh_key, fresh_value = triple
 
     scale = 1.0 / math.sqrt(HEAD_DIM)
-    spread = jnp.where(head_mask, matmul(expand, query), 0.0).astype(BF16)
+    spread = jnp.where(head_mask, matmul(expand, projected(0)), 0.0).astype(BF16)
     scores = matmul_nt(spread, kv[...].reshape(slots * ctx, width)) * scale
     own = (
         jnp.sum(
-            jnp.where(expand_mask, matmul_nt(spread, fresh_key), 0.0), axis=1, keepdims=True
+            jnp.where(expand_mask, matmul_nt(spread, projected(1)), 0.0), axis=1, keepdims=True
         )
         * scale
     )
@@ -267,7 +302,7 @@
     weights = (probs / total).astype(BF16)
     self_weight = (self_prob / total).astype(BF16).astype(F32)
     mixed = matmul(weights, vv[...].reshape(slots * ctx, width))
-    mixed = mixed + self_weight * matmul(expand, fresh_value)
+    mixed = mixed + self_weight * matmul(expand, projected(2))
     mixed = jnp.where(head_mask, mixed, 0.0).astype(BF16)
     hbuf[me_g] = matmul(collapse, mixed).astype(BF16)
     copies = [
@@ -282,43 +317,48 @@
     heads_out = hbuf[...].astype(F32).reshape(batch, width).astype(BF16)
     heads_out = matmul_tn(to_slots, heads_out).astype(BF16)
 
-    ocols = min(COLUMNS, feat)
-
-    def out_step(c, carry):
-        at = pl.ds(pl.multiple_of(c * ocols, ocols), ocols)
-        term = matmul(heads_out, wo[:, at])
+    pieces, ocols = obuf.shape[0], obuf.shape[3]
+    o_copies, a_out = [], []
+    for p in range(pieces):
+        term = matmul(heads_out, wo[:, p * ocols : (p + 1) * ocols])
         for t in range(nt):
-            obuf[t, :, at] = term[t * xb : (t + 1) * xb].astype(BF16)
-        return carry
-
-    lax.fori_loop(0, feat // ocols, out_step, 0)
-    copies = [
-        remote(obuf.at[t_peer(k)], robuf.at[k - 1], o_sems, (k - 1,), t_id(k))
-        for k in range(1, nt)
-    ]
-    for c in copies:
-        c.start()
-    pending += copies
-    for c in copies:
-        c.wait_recv()
-    head_sums = obuf[me_t].astype(F32)
-    for k in range(nt - 1):
-        head_sums = head_sums + robuf[k].astype(F32)
-    attended = (xv[...].astype(F32) + head_sums).astype(BF16)
-    att_ref[...] = attended
-    abuf[me_t] = attended
-    copies = [
-        remote(abuf.at[me_t], abuf.at[me_t], a_sems, (k - 1,), t_id(k)) for k in range(1, nt)
-    ]
-    for c in copies:
-        c.start()
-    pending += copies
+            obuf[p, t] = term[t * xb : (t + 1) * xb].astype(BF16)
+        step = [
+            remote(obuf.at[p, t_peer(k)], robuf.at[p, k - 1], o_sems, (p, k - 1), t_id(k))
+            for k in range(1, nt)
+        ]
+        for c in step:
+            c.start()
+        o_copies.append(step)
+        pending += step
+    for p in range(pieces):
+        for c in o_copies[p]:
+            c.wait_recv()
+        head_sums = obuf[p, me_t].astype(F32)
+        for k in range(nt - 1):
+            head_sums = head_sums + robuf[p, k].astype(F32)
+        at = slice(p * ocols, (p + 1) * ocols)
+        attended = (xv[:, at].astype(F32) + head_sums).astype(BF16)
+        att_ref[:, at] = attended
+        abuf[p, me_t] = attended
+        step = [
+            remote(abuf.at[p, me_t], abuf.at[p, me_t], a_sems, (p, k - 1), t_id(k))
+            for k in range(1, nt)
+        ]
+        for c in step:
+            c.start()
+        a_out.append(step)
+        pending += step
     small[2].wait()
-    for c in copies:
-        c.wait_recv()
-
-    wide = abuf[...].astype(F32).reshape(batch, feat)
-    squares = jnp.sum(wide * wide, axis=1, keepdims=True)
+
+    gained, squares = [], 0.0
+    for p in range(pieces):
+        for c in a_out[p]:
+            c.wait_recv()
+        wide = abuf[p].astype(F32).reshape(batch, ocols)
+        squares = squares + jnp.sum(wide * wide, axis=1, keepdims=True)
+        gained.append((wide * mgainv[:, p * ocols : (p + 1) * ocols]).astype(BF16))
+    gained = jnp.concatenate(gained, axis=1)
     for g in range(ng):
         msq_send[g] = jnp.broadcast_to(squares[g * slots : (g + 1) * slots], msq_send.shape[1:])
     msq_copies = [
@@ -328,7 +368,6 @@
     for c in msq_copies:
         c.start()
     pending += msq_copies
-    gained = (wide * mgainv[...]).astype(BF16)
 
     m_steps = []
     for j in range(3):
@@ -409,6 +448,9 @@
     vmem = pl.BlockSpec(memory_space=pltpu.VMEM)
     dma = pltpu.SemaphoreType.DMA
     others_g, others_t = max(ng - 1, 1), max(nt - 1, 1)
+    others_r, others_c = max(nr - 1, 1), max(nc - 1, 1)
+    ocols = math.gcd(COLUMNS, feat)
+    pieces = feat // ocols
     weight_values = attn_proj.size + out_proj.size + mix_proj.size
     return pl.pallas_call(
         functools.partial(kernel, nt, nr, nc),
@@ -434,12 +476,15 @@
             pltpu.VMEM((xb, LANES), F32),
             pltpu.VMEM((others_g, xb, LANES), F32),
             pltpu.VMEM((nt, xb, feat), BF16),
-            pltpu.VMEM((ng, 3, slots, width), F32),
-            pltpu.VMEM((others_g, 3, slots, width), F32),
+            pltpu.VMEM((nt, xb, LANES), F32),
+            pltpu.VMEM((3, nc, nr, slots, width), F32),
+            pltpu.VMEM((others_c, 3, nr, slots, width), F32),
+            pltpu.VMEM((3, nr, slots, width), F32),
+            pltpu.VMEM((others_r, 3, slots, width), F32),
             pltpu.VMEM((ng, slots, width), BF16),
-            pltpu.VMEM((nt, xb, feat), BF16),
-            pltpu.VMEM((others_t, xb, feat), BF16),
-            pltpu.VMEM((nt, xb, feat), BF16),
+            pltpu.VMEM((pieces, nt, xb, ocols), BF16),
+            pltpu.VMEM((pieces, others_t, xb, ocols), BF16),
+            pltpu.VMEM((pieces, nt, xb, ocols), BF16),
             pltpu.VMEM((ng, slots, LANES), F32),
             pltpu.VMEM((others_g, slots, LANES), F32),
             pltpu.VMEM((ng, 3, slots, width), BF16),
@@ -448,10 +493,12 @@
             dma((7,)),
             dma((2, others_g)),
             dma((2, others_t)),
-            dma((2, others_g, 3)),
+            dma((2, others_t)),
+            dma((2, others_c, 3)),
+            dma((2, others_r, 3)),
             dma((2, others_g)),
-            dma((2, others_t)),
-            dma((2, others_t)),
+            dma((2, pieces, others_t)),
+            dma((2, pieces, others_t)),
             dma((2, others_g)),
             dma((2, others_g, 3)),
         ],

time: 56.1 us -> 47.9 us (0.85)
  Pallas kernels: 52.5 us -> 44.2 us
    pallas_call x1, Pallas kernels: 52.5 us -> 44.2 us  [local(): pl.pallas_call(functools.partial(kernel, nt, nr, nc), out_shape=(jax.Shap...]
where the time goes in v2:
time: 47.9 us; the launch traced here: 47.6 us
  Pallas kernels  44.2 us (92%)
  local copies, waits for them, and re-layouts  2.75 us (6%)
  between operations  0.64 us (1%)
    pallas_call x1, Pallas kernels, local(): pl.pallas_call(functools.partial(kernel, nt, nr, nc), out_shape=(jax.Shap...  44.2 us
    unnamed x2, local copies, waits for them, and re-layouts  2.75 us

profile of v2, /device:TPU:0, one launch (start us, length us, event | category | flops | bytes accessed | tf_op | source)
XLA Modules:
  0.0 47.6 jit_solution(3483901321709445933)
XLA Ops:
  0.6 44.2 %hybrid_block.1 = (bf16[8,2048]{1,0:T(8,128)(2,1)}, bf16[8,2048]{1,0:T(8,128)(2,1)}) custom-call(bf16[8,2048]{1,0:T(8,128)(2,1)} %x_hbm.1, f32[1,2048]{1,0:T(1,128)} %bitcast.4, bf16[3,2048,2048]{2,1,0:T(8,128)(2,1)} %aproj_hbm.1, bf16[8,32,2048]{2,1,0:T(8,128)(2,1)} %keys_hbm.1, bf16[8,32,2048]{2,1,0:T(8,128)(2,1)} %vals_hbm.1, s32[1,8]{1,0:T(1,128)} %bitcast.6, ...), custom_call_target="tpu_custom_call" | custom-call | flops 1879048192 | bytes 58720256 | tf_op jit(solution)/shard_map/hybrid_block/pallas_call | solution.py:455
  44.8 1.4 %copy.18 = bf16[8,2048]{1,0:T(8,128)(2,1)} copy(bf16[8,2048]{1,0:T(8,128)(2,1)} %get-tuple-element.4) | data formatting | bytes 65536
  46.2 1.4 %copy.19 = bf16[8,2048]{1,0:T(8,128)(2,1)} copy(bf16[8,2048]{1,0:T(8,128)(2,1)} %get-tuple-element.5) | data formatting | bytes 65536

commit v3 on v2

--- a/solution.py
+++ b/solution.py
@@ -88,7 +88,10 @@
     abuf,
     msq_send,
     msq_recv,
+    macc,
     mbuf,
+    mcbuf,
+    msbuf,
     rmbuf,
     lsem,
     wsem,
@@ -101,6 +104,7 @@
     o_sems,
     a_sems,
     msq_sems,
+    mc_sems,
     m_sems,
 ):
     ng = nr * nc
@@ -351,44 +355,86 @@
         pending += step
     small[2].wait()
 
-    gained, squares = [], 0.0
+    def mix_weight(j):
+        return wm if j == 0 else wa.at[j - 1]
+
+    def cross_chips(j):
+        for c in mc_copies[j]:
+            c.wait_recv()
+        total = mbuf[j, me_c].astype(F32)
+        for k in range(nc - 1):
+            total = total + mcbuf[k, j].astype(F32)
+        msbuf[j] = total.astype(BF16)
+        step = [
+            remote(
+                msbuf.at[j, r_peer(k)], rmbuf.at[k - 1, j], m_sems, (k - 1, j), {"rows": r_peer(k)}
+            )
+            for k in range(1, nr)
+        ]
+        for c in step:
+            c.start()
+        return step
+
+    squares = 0.0
+    mc_copies, m_steps = [], []
     for p in range(pieces):
         for c in a_out[p]:
             c.wait_recv()
+        depth = slice(p * ocols, (p + 1) * ocols)
         wide = abuf[p].astype(F32).reshape(batch, ocols)
         squares = squares + jnp.sum(wide * wide, axis=1, keepdims=True)
-        gained.append((wide * mgainv[:, p * ocols : (p + 1) * ocols]).astype(BF16))
-    gained = jnp.concatenate(gained, axis=1)
-    for g in range(ng):
-        msq_send[g] = jnp.broadcast_to(squares[g * slots : (g + 1) * slots], msq_send.shape[1:])
-    msq_copies = [
-        remote(msq_send.at[g_peer(k)], msq_recv.at[k - 1], msq_sems, (k - 1,), g_id(k))
-        for k in range(1, ng)
-    ]
-    for c in msq_copies:
-        c.start()
-    pending += msq_copies
-
-    m_steps = []
-    for j in range(3):
-        m_copies[j].wait()
-
-        def mix_step(c, carry, j=j):
-            at = pl.ds(pl.multiple_of(c * cols, cols), cols)
-            weight = wm[:, at] if j == 0 else wa[j - 1, :, at]
-            term = matmul(gained, weight)
+        gained = (wide * mgainv[:, depth]).astype(BF16)
+        last = p == pieces - 1
+        if last:
             for g in range(ng):
-                mbuf[g, j, :, at] = term[g * slots : (g + 1) * slots].astype(BF16)
-            return carry
-
-        lax.fori_loop(0, width // cols, mix_step, 0)
-        step = [
-            remote(mbuf.at[g_peer(k), j], rmbuf.at[k - 1, j], m_sems, (k - 1, j), g_id(k))
-            for k in range(1, ng)
-        ]
-        for c in step:
-            c.start()
-        m_steps.append(step)
+                msq_send[g] = jnp.broadcast_to(
+                    squares[g * slots : (g + 1) * slots], msq_send.shape[1:]
+                )
+            msq_copies = [
+                remote(msq_send.at[g_peer(k)], msq_recv.at[k - 1], msq_sems, (k - 1,), g_id(k))
+                for k in range(1, ng)
+            ]
+            for c in msq_copies:
+                c.start()
+            pending += msq_copies
+        for j in range(3):
+            if p == 0:
+                m_copies[j].wait()
+
+            def mix_step(c, carry, p=p, j=j, last=last, depth=depth, gained=gained):
+                at = pl.ds(pl.multiple_of(c * cols, cols), cols)
+                term = matmul(gained, mix_weight(j)[depth, at])
+                if p > 0:
+                    term = term + macc[j, :, at]
+                if last:
+                    for g in range(ng):
+                        mbuf[j, g % nc, g // nc, :, at] = term[
+                            g * slots : (g + 1) * slots
+                        ].astype(BF16)
+                else:
+                    macc[j, :, at] = term
+                return carry
+
+            lax.fori_loop(0, width // cols, mix_step, 0)
+            if last:
+                step = [
+                    remote(
+                        mbuf.at[j, c_peer(k)],
+                        mcbuf.at[k - 1, j],
+                        mc_sems,
+                        (k - 1, j),
+                        {"role": c_peer(k)},
+                    )
+                    for k in range(1, nc)
+                ]
+                for c in step:
+                    c.start()
+                mc_copies.append(step)
+                pending += step
+                if j > 0:
+                    m_steps.append(cross_chips(j - 1))
+    m_steps.append(cross_chips(2))
+    for step in m_steps:
         pending += step
 
     for c in small[5:]:
@@ -403,8 +449,8 @@
     for j in range(3):
         for c in m_steps[j]:
             c.wait_recv()
-        total = mbuf[me_g, j].astype(F32)
-        for k in range(ng - 1):
+        total = msbuf[j, me_r].astype(F32)
+        for k in range(nr - 1):
             total = total + rmbuf[k, j].astype(F32)
         conv.append(
             otv[0, j : j + 1] * (total * scale_rows)
@@ -418,6 +464,17 @@
     gated_ref[...] = (conv[1] * filtered).astype(BF16)
     for c in pending:
         c.wait_send()
+
+
+def hand_over(att_in, gated_in, att_out, gated_out, sems):
+    copies = [
+        pltpu.make_async_copy(att_in, att_out, sems.at[0]),
+        pltpu.make_async_copy(gated_in, gated_out, sems.at[1]),
+    ]
+    for c in copies:
+        c.start()
+    for c in copies:
+        c.wait()
 
 
 def local(
@@ -452,7 +509,7 @@
     ocols = math.gcd(COLUMNS, feat)
     pieces = feat // ocols
     weight_values = attn_proj.size + out_proj.size + mix_proj.size
-    return pl.pallas_call(
+    attended, gated = pl.pallas_call(
         functools.partial(kernel, nt, nr, nc),
         out_shape=(
             jax.ShapeDtypeStruct((xb, feat), BF16),
@@ -487,8 +544,11 @@
             pltpu.VMEM((pieces, nt, xb, ocols), BF16),
             pltpu.VMEM((ng, slots, LANES), F32),
             pltpu.VMEM((others_g, slots, LANES), F32),
-            pltpu.VMEM((ng, 3, slots, width), BF16),
-            pltpu.VMEM((others_g, 3, slots, width), BF16),
+            pltpu.VMEM((3, batch, width), F32),
+            pltpu.VMEM((3, nc, nr, slots, width), BF16),
+            pltpu.VMEM((others_c, 3, nr, slots, width), BF16),
+            pltpu.VMEM((3, nr, slots, width), BF16),
+            pltpu.VMEM((others_r, 3, slots, width), BF16),
             dma((9,)),
             dma((7,)),
             dma((2, others_g)),
@@ -500,7 +560,8 @@
             dma((2, pieces, others_t)),
             dma((2, pieces, others_t)),
             dma((2, others_g)),
-            dma((2, others_g, 3)),
+            dma((2, others_c, 3)),
+            dma((2, others_r, 3)),
         ],
         compiler_params=pltpu.CompilerParams(
             collective_id=0, has_side_effects=True, vmem_limit_bytes=58 * 2**20
@@ -525,6 +586,17 @@
         inner_taps,
         inner_state,
     )
+    return pl.pallas_call(
+        hand_over,
+        out_shape=(
+            jax.ShapeDtypeStruct((xb, feat), BF16),
+            jax.ShapeDtypeStruct((slots, width), BF16),
+        ),
+        in_specs=[anywhere] * 2,
+        out_specs=(anywhere, anywhere),
+        scratch_shapes=[dma((2,))],
+        name="hand_over",
+    )(attended, gated)
 
 
 def solution(mesh):

time: 47.9 us -> 49.3 us (1.029)
  Pallas kernels: 44.2 us -> 48.4 us
  local copies, waits for them, and re-layouts: 2.75 us -> 0 us
    pallas_call x0 -> x1, Pallas kernels: none -> 3.11 us  [local(): pl.pallas_call(hand_over, out_shape=(jax.ShapeDtypeStruct((xb, feat), BF1...]
    unnamed x2 -> x0, local copies, waits for them, and re-layouts: 2.75 us -> none
    pallas_call x1, Pallas kernels: 44.2 us -> 45.3 us  [local(): pl.pallas_call(functools.partial(kernel, nt, nr, nc), out_shape=(jax.Shap...]
where the time goes in v3:
time: 49.3 us; the launch traced here: 49.1 us
  Pallas kernels  48.4 us (98%)
  between operations  0.64 us (1%)
    pallas_call x1, Pallas kernels, local(): pl.pallas_call(functools.partial(kernel, nt, nr, nc), out_shape=(jax.Shap...  45.3 us
    pallas_call x1, Pallas kernels, local(): pl.pallas_call(hand_over, out_shape=(jax.ShapeDtypeStruct((xb, feat), BF1...  3.11 us

profile of v3, /device:TPU:0, one launch (start us, length us, event | category | flops | bytes accessed | tf_op | source)
XLA Modules:
  0.0 49.1 jit_solution(9727536770212454654)
XLA Ops:
  0.6 45.3 %hybrid_block.1 = (bf16[8,2048]{1,0:T(8,128)(2,1)}, bf16[8,2048]{1,0:T(8,128)(2,1)}) custom-call(bf16[8,2048]{1,0:T(8,128)(2,1)} %x_hbm.1, f32[1,2048]{1,0:T(1,128)} %bitcast.4, bf16[3,2048,2048]{2,1,0:T(8,128)(2,1)} %aproj_hbm.1, bf16[8,32,2048]{2,1,0:T(8,128)(2,1)} %keys_hbm.1, bf16[8,32,2048]{2,1,0:T(8,128)(2,1)} %vals_hbm.1, s32[1,8]{1,0:T(1,128)} %bitcast.6, ...), custom_call_target="tpu_custom_call" | custom-call | flops 1879048192 | bytes 58720256 | tf_op jit(solution)/shard_map/hybrid_block/pallas_call | solution.py:512
  46.0 3.1 %hand_over.1 = (bf16[8,2048]{1,0:T(8,128)(2,1)}, bf16[8,2048]{1,0:T(8,128)(2,1)}) custom-call(bf16[8,2048]{1,0:T(8,128)(2,1)} %get-tuple-element.4.att_in, bf16[8,2048]{1,0:T(8,128)(2,1)} %get-tuple-element.5.gated_in), custom_call_target="tpu_custom_call" | custom-call | tf_op jit(solution)/shard_map/hand_over/pallas_call | solution.py:589

commit v4 on v2

--- a/solution.py
+++ b/solution.py
@@ -236,13 +236,14 @@
         a_copies[j].wait()
 
         def attn_step(c, carry, j=j):
-            at = pl.ds(pl.multiple_of(c * cols, cols), cols)
+            at = slice(c * cols, (c + 1) * cols)
             term = matmul(normed, wa[j, :, at])
             for g in range(ng):
                 tbuf[j, g % nc, g // nc, :, at] = term[g * slots : (g + 1) * slots]
             return carry
 
-        lax.fori_loop(0, width // cols, attn_step, 0)
+        for c in range(width // cols):
+            attn_step(c, 0)
         if j < 2:
             m_copies[1 + j].start()
         step = [
@@ -373,23 +374,24 @@
     for j in range(3):
         m_copies[j].wait()
 
-        def mix_step(c, carry, j=j):
-            at = pl.ds(pl.multiple_of(c * cols, cols), cols)
+        step = []
+        for i in range(width // cols):
+            at = slice(i * cols, (i + 1) * cols)
             weight = wm[:, at] if j == 0 else wa[j - 1, :, at]
             term = matmul(gained, weight)
             for g in range(ng):
-                mbuf[g, j, :, at] = term[g * slots : (g + 1) * slots].astype(BF16)
-            return carry
-
-        lax.fori_loop(0, width // cols, mix_step, 0)
-        step = [
-            remote(mbuf.at[g_peer(k), j], rmbuf.at[k - 1, j], m_sems, (k - 1, j), g_id(k))
-            for k in range(1, ng)
-        ]
-        for c in step:
-            c.start()
+                mbuf[j, i, g] = term[g * slots : (g + 1) * slots].astype(BF16)
+            piece = [
+                remote(
+                    mbuf.at[j, i, g_peer(k)], rmbuf.at[j, i, k - 1], m_sems, (k - 1, j, i), g_id(k)
+                )
+                for k in range(1, ng)
+            ]
+            for c in piece:
+                c.start()
+            step.append(piece)
+            pending += piece
         m_steps.append(step)
-        pending += step
 
     for c in small[5:]:
         c.wait()
@@ -401,11 +403,15 @@
     scale_rows = lax.rsqrt(squares[:, :1] / total_feat + 1e-05)
     conv = []
     for j in range(3):
-        for c in m_steps[j]:
-            c.wait_recv()
-        total = mbuf[me_g, j].astype(F32)
-        for k in range(ng - 1):
-            total = total + rmbuf[k, j].astype(F32)
+        total = []
+        for i, piece in enumerate(m_steps[j]):
+            for c in piece:
+                c.wait_recv()
+            part = mbuf[j, i, me_g].astype(F32)
+            for k in range(ng - 1):
+                part = part + rmbuf[j, i, k].astype(F32)
+            total.append(part)
+        total = jnp.concatenate(total, axis=1)
         conv.append(
             otv[0, j : j + 1] * (total * scale_rows)
             + otv[1, j : j + 1] * osv[0, j].astype(F32)
@@ -449,7 +455,7 @@
     dma = pltpu.SemaphoreType.DMA
     others_g, others_t = max(ng - 1, 1), max(nt - 1, 1)
     others_r, others_c = max(nr - 1, 1), max(nc - 1, 1)
-    ocols = math.gcd(COLUMNS, feat)
+    ocols, wcols = math.gcd(COLUMNS, feat), math.gcd(COLUMNS, width)
     pieces = feat // ocols
     weight_values = attn_proj.size + out_proj.size + mix_proj.size
     return pl.pallas_call(
@@ -487,8 +493,8 @@
             pltpu.VMEM((pieces, nt, xb, ocols), BF16),
             pltpu.VMEM((ng, slots, LANES), F32),
             pltpu.VMEM((others_g, slots, LANES), F32),
-            pltpu.VMEM((ng, 3, slots, width), BF16),
-            pltpu.VMEM((others_g, 3, slots, width), BF16),
+            pltpu.VMEM((3, width // wcols, ng, slots, wcols), BF16),
+            pltpu.VMEM((3, width // wcols, others_g, slots, wcols), BF16),
             dma((9,)),
             dma((7,)),
             dma((2, others_g)),
@@ -500,7 +506,7 @@
             dma((2, pieces, others_t)),
             dma((2, pieces, others_t)),
             dma((2, others_g)),
-            dma((2, others_g, 3)),
+            dma((2, others_g, 3, width // wcols)),
         ],
         compiler_params=pltpu.CompilerParams(
             collective_id=0, has_side_effects=True, vmem_limit_bytes=58 * 2**20

time: 47.9 us -> 47.5 us (level)
  no operation moved by 1% of the time
where the time goes in v4:
time: 47.5 us; the launch traced here: 47.3 us
  Pallas kernels  43.9 us (92%)
  local copies, waits for them, and re-layouts  2.75 us (6%)
  between operations  0.64 us (1%)
    pallas_call x1, Pallas kernels, local(): pl.pallas_call(functools.partial(kernel, nt, nr, nc), out_shape=(jax.Shap...  43.9 us
    unnamed x2, local copies, waits for them, and re-layouts  2.75 us

profile of v4, /device:TPU:0, one launch (start us, length us, event | category | flops | bytes accessed | tf_op | source)
XLA Modules:
  0.0 47.3 jit_solution(9697525377538760864)
XLA Ops:
  0.6 43.9 %hybrid_block.1 = (bf16[8,2048]{1,0:T(8,128)(2,1)}, bf16[8,2048]{1,0:T(8,128)(2,1)}) custom-call(bf16[8,2048]{1,0:T(8,128)(2,1)} %x_hbm.1, f32[1,2048]{1,0:T(1,128)} %bitcast.4, bf16[3,2048,2048]{2,1,0:T(8,128)(2,1)} %aproj_hbm.1, bf16[8,32,2048]{2,1,0:T(8,128)(2,1)} %keys_hbm.1, bf16[8,32,2048]{2,1,0:T(8,128)(2,1)} %vals_hbm.1, s32[1,8]{1,0:T(1,128)} %bitcast.6, ...), custom_call_target="tpu_custom_call" | custom-call | flops 1879048192 | bytes 58720256 | tf_op jit(solution)/shard_map/hybrid_block/pallas_call | solution.py:461
  44.5 1.4 %copy.18 = bf16[8,2048]{1,0:T(8,128)(2,1)} copy(bf16[8,2048]{1,0:T(8,128)(2,1)} %get-tuple-element.4) | data formatting | bytes 65536
  45.9 1.4 %copy.19 = bf16[8,2048]{1,0:T(8,128)(2,1)} copy(bf16[8,2048]{1,0:T(8,128)(2,1)} %get-tuple-element.5) | data formatting | bytes 65536
